TPU v7x, 32 devices: a whole 2x2x4 slice. The times are simulated.
32 devices in a mesh: section: 2 (over x), dp: 16 (over z, y, core).
Axes of the slice: x: 2, y: 2, z: 4, core: 2. Of those that a mesh axis runs over, the one named last changes fastest.
Arguments:
- x_input: bfloat16 [16384, 768], P('dp'), may hold values from -6 to 6
- w_qkv: bfloat16 [2, 768, 2304], P('section'), may hold values from -0.21875 to 0.21875
- bias_query: float32 [2, 768], P('section'), may hold values from -4 to 4
- bias_value: float32 [2, 768], P('section'), may hold values from -1.5 to 1.5
- w_out: bfloat16 [2, 768, 768], P('section'), may hold values from -0.875 to 0.875
- bias_out: float32 [2, 768], P('section'), may hold values from -1.5 to 1.5
- gain_attn: float32 [2, 768], P('section'), may hold values from 0.5 to 1.5
- shift_attn: float32 [2, 768], P('section'), may hold values from -3 to 3
- w_in: bfloat16 [2, 768, 3072], P('section'), may hold values from -0.21875 to 0.21875
- bias_in: float32 [2, 3072], P('section'), may hold values from -1.5 to 1.5
- w_back: bfloat16 [2, 3072, 768], P('section'), may hold values from -0.109375 to 0.109375
- bias_back: float32 [2, 768], P('section'), may hold values from -1.5 to 1.5
- gain_ffn: float32 [2, 768], P('section'), may hold values from 0.5 to 1.5
- shift_ffn: float32 [2, 768], P('section'), may hold values from -3 to 3
- lengths: int32 [32], P('dp'), may hold values from 160 to 512, as said below
- cotangent: bfloat16 [16384, 768], P('dp'), may hold values from -6 to 6
Outputs:
- activations: bfloat16 [2, 16384, 768], P('section', 'dp')
- input_grads: float32 [2, 16384, 768], P('section', 'dp')
- grad_w_qkv: float32 [2, 768, 2304], P('section')
- grad_bias_query: float32 [2, 768], P('section')
- grad_bias_value: float32 [2, 768], P('section')
- grad_w_out: float32 [2, 768, 768], P('section')
- grad_bias_out: float32 [2, 768], P('section')
- grad_gain_attn: float32 [2, 768], P('section')
- grad_shift_attn: float32 [2, 768], P('section')
- grad_w_in: float32 [2, 768, 3072], P('section')
- grad_bias_in: float32 [2, 3072], P('section')
- grad_w_back: float32 [2, 3072, 768], P('section')
- grad_bias_back: float32 [2, 768], P('section')
- grad_gain_ffn: float32 [2, 768], P('section')
- grad_shift_ffn: float32 [2, 768], P('section')
Inputs may be any that keep to these rules, and one draw needn't show every extreme that they name: Passage lengths in tokens; some passage is exactly 512 long.
All inputs are finite; a program needn't handle non-finite values.
Results may differ from a plain program's by a relative error of at most 0.022.
Values may be sent and summed in bfloat16 or wider, within the bound.
A program may use at most 320 MiB of HBM per device.

v0:
```python
import functools

import jax
import jax.numpy as jnp
from jax import lax
from jax.experimental import pallas as pl
from jax.experimental.pallas import tpu as pltpu
from jax.sharding import PartitionSpec as P

HEAD = 64
LANES = 128
MB = 2
EPSILON = 1e-12
DEAD = -1e30
FACTOR_ATTN = 12
FACTOR_FFN = 13
STAT_COLUMNS = 16
VMEM_LIMIT = 62 << 20

FORWARD_VECTORS = (
    "bias_query",
    "bias_value",
    "bias_out",
    "gain_attn",
    "shift_attn",
    "bias_in",
    "bias_back",
    "gain_ffn",
    "shift_ffn",
)
SUM_ROWS = tuple(name for name in FORWARD_VECTORS if name != "bias_in")
SUM_COUNT = 16

f32 = jnp.float32
bf16 = jnp.bfloat16
MESH = pl.DeviceIdType.MESH
NN = (((1,), (0,)), ((), ()))
NT = (((1,), (1,)), ((), ()))
TN = (((0,), (0,)), ((), ()))


def mm(left, right, dims=NN):
    return lax.dot_general(left, right, dims, preferred_element_type=f32)


def rows_at(index, count):
    return pl.ds(pl.multiple_of(index * count, count), count)


def norm_rows(value):
    centred = value - jnp.mean(value, axis=-1, keepdims=True)
    factor = lax.rsqrt(jnp.mean(centred * centred, axis=-1, keepdims=True) + EPSILON)
    return centred * factor, factor


def norm_back(grad_hat, unit, factor):
    return factor * (
        grad_hat
        - jnp.mean(grad_hat, axis=-1, keepdims=True)
        - unit * jnp.mean(grad_hat * unit, axis=-1, keepdims=True)
    )


def column_sum(value):
    return jnp.sum(value, axis=0, keepdims=True)


def split_three(value):
    high = value.astype(bf16)
    rest = value - high.astype(f32)
    middle = rest.astype(bf16)
    low = (rest - middle.astype(f32)).astype(bf16)
    return high, middle, low


def key_bias(rows, length):
    key = lax.broadcasted_iota(jnp.int32, (rows, LANES), 0)
    return jnp.where(key < length, 0.0, DEAD).astype(bf16)


def attention_forward(qkv, mixed, stats, length, width):
    rows = qkv.shape[0]
    heads = width // HEAD
    lane = lax.broadcasted_iota(jnp.int32, (rows, LANES), 1)
    dead = key_bias(rows, length)
    zero = jnp.zeros((rows, LANES), bf16)
    one = jnp.ones((rows, LANES), bf16)

    def marked(part, head, mark):
        value = qkv[:, pl.ds(part * width + head // 2 * LANES, LANES)]
        own = (lane < HEAD) if head % 2 == 0 else (lane >= HEAD)
        return jnp.where(own, value, jnp.where(lane == HEAD - HEAD * (head % 2), mark, zero))

    def scores_of(head):
        return mm(marked(1, head, dead), marked(0, head, one), NT)

    ahead = [scores_of(0), scores_of(1)]
    outs, log_totals = [], []
    for head in range(heads):
        if head + 2 < heads:
            ahead.append(scores_of(head + 2))
        scores = ahead[head]
        ahead[head] = None
        highest = jnp.max(scores, axis=0, keepdims=True)
        weights = jnp.exp(scores - highest).astype(bf16)
        product = mm(marked(2, head, one).T, weights)
        odd = head % 2
        total = product[HEAD - HEAD * odd : HEAD - HEAD * odd + 1]
        outs.append(product[HEAD * odd : HEAD * odd + HEAD] * (1.0 / total))
        log_totals.append(highest + jnp.log(total))
        if odd:
            mixed[:, pl.ds(head // 2 * LANES, LANES)] = jnp.concatenate(outs, 0).T.astype(bf16)
            outs = []
    spare = STAT_COLUMNS - heads
    log_totals = jnp.concatenate(log_totals + [jnp.zeros((spare, rows), f32)], 0)
    stats[:, :STAT_COLUMNS] = log_totals.T


def forward_block(weights, vec, need, length, saved, unit1, unit2, result, send, done):
    w_qkv, w_out, w_in, w_back = weights
    x, qkv, mixed, stats, slope, active, normed = saved
    rows, width = x.shape
    half_rows = rows // 2
    scale = HEAD ** -0.5
    need("query")
    qkv[:, :width] = ((mm(x[...], w_qkv[:, :width]) + vec["bias_query"][...]) * scale).astype(bf16)
    need("key")
    qkv[:, width : 2 * width] = mm(x[...], w_qkv[:, width : 2 * width]).astype(bf16)
    qkv[:, 2 * width :] = (mm(x[...], w_qkv[:, 2 * width :]) + vec["bias_value"][...]).astype(bf16)
    attention_forward(qkv, mixed, stats, length, width)
    lane = lax.broadcasted_iota(jnp.int32, (half_rows, LANES), 1)
    need("out")

    def after_attention(block, carry):
        rs = rows_at(block, half_rows)
        summed = x[rs, :].astype(f32) + mm(mixed[rs, :], w_out[...]) + vec["bias_out"][...]
        unit, factor = norm_rows(summed)
        unit1[rs, :] = unit
        normed[rs, :] = (unit * vec["gain_attn"][...] + vec["shift_attn"][...]).astype(bf16)
        stats[rs, :] = jnp.where(lane == FACTOR_ATTN, factor, stats[rs, :])
        return carry

    lax.fori_loop(0, 2, after_attention, 0)
    done("attn")
    need("in")

    def hidden(j, carry):
        cs = rows_at(j, width)
        inner = mm(normed[...], w_in[:, cs]) + vec["bias_in"][:, cs]
        share = 0.5 * (1.0 + lax.erf(inner * 0.7071067811865476))
        active[:, cs] = (inner * share).astype(bf16)
        slope[:, cs] = (
            share + inner * jnp.exp(-0.5 * inner * inner) * 0.3989422804014327
        ).astype(bf16)
        return carry

    lax.fori_loop(0, w_in.shape[1] // width, hidden, 0)
    need("back")

    def after_ffn(block, carry):
        rs = rows_at(block, half_rows)
        summed = normed[rs, :].astype(f32) + mm(active[rs, :], w_back[...]) + vec["bias_back"][...]
        unit, factor = norm_rows(summed)
        unit2[rs, :] = unit
        result[rs, :] = (unit * vec["gain_ffn"][...] + vec["shift_ffn"][...]).astype(bf16)
        stats[rs, :] = jnp.where(lane == FACTOR_FFN, factor, stats[rs, :])
        send(block)
        return carry

    lax.fori_loop(0, 2, after_ffn, 0)
    done("ffn")


def attention_backward(qkv, gmix, mixed, stats, length, width, sums, between):
    rows = qkv.shape[0]
    heads = width // HEAD
    lane = lax.broadcasted_iota(jnp.int32, (rows, LANES), 1)
    dead = key_bias(rows, length)
    zero = jnp.zeros((rows, LANES), bf16)
    one = jnp.ones((rows, LANES), bf16)

    def operands(head):
        cols = [pl.ds(part * width + head // 2 * LANES, LANES) for part in range(3)]
        q2, k2, v2 = [qkv[:, c] for c in cols]
        g2 = gmix[:, cols[0]]
        own = (lane < HEAD) if head % 2 == 0 else (lane >= HEAD)
        at = HEAD - HEAD * (head % 2)
        terms = jnp.where(own, g2.astype(f32) * mixed[:, cols[0]].astype(f32), 0.0)
        d0, d1, d2 = split_three(-jnp.sum(terms, axis=-1, keepdims=True))
        l0, l1, l2 = split_three(-stats[:, head : head + 1])
        m0, m1, m2, m3 = [lane == at + t for t in range(4)]
        m012 = m0 | m1 | m2
        qa = jnp.where(
            own,
            q2,
            jnp.where(m0, l0, jnp.where(m1, l1, jnp.where(m2, l2, jnp.where(m3, one, zero)))),
        )
        ga = jnp.where(own, g2, jnp.where(m0, d0, jnp.where(m1, d1, jnp.where(m2, d2, zero))))
        ka = jnp.where(own, k2, jnp.where(m012, one, jnp.where(m3, dead, zero)))
        va = jnp.where(own, v2, jnp.where(m012, one, zero))
        first = HEAD * (head % 2)
        return q2, g2, k2.T[first : first + HEAD], mm(ka, qa, NT), mm(va, ga, NT)

    ahead = operands(0)
    grads = []
    for head in range(heads):
        q2, g2, k2_t, scores, grad_probs = ahead
        if head + 1 < heads:
            ahead = operands(head + 1)
        probs = jnp.exp(scores)
        grad_scores = (probs * grad_probs).astype(bf16)
        grads.append((mm(k2_t, grad_scores), mm(grad_scores, q2), mm(probs.astype(bf16), g2)))
        if head % 2:
            pair = head // 2
            even, odd = grads
            grads = []
            grad_q = jnp.concatenate([even[0], odd[0]], 0).T * (HEAD ** -0.5)
            grad_k = jnp.where(lane < HEAD, even[1], odd[1])
            grad_v = jnp.where(lane < HEAD, even[2], odd[2])
            for part, grad in enumerate((grad_q, grad_k, grad_v)):
                qkv[:, pl.ds(part * width + pair * LANES, LANES)] = grad.astype(bf16)
            cols = pl.ds(pair * LANES, LANES)
            sums["bias_query"][:, cols] += column_sum(grad_q)
            sums["bias_value"][:, cols] += column_sum(grad_v)
            between(pair)


def backward_block(grad_of, unit_of, weights, vec, need, length, saved, work, sums, give, hook):
    w_qkv, w_out, w_in, w_back = weights
    qkv, mixed, stats, slope = saved
    unit, gouter, gatt, gmix, gsum = work
    rows, width = gsum.shape
    half_rows = rows // 2
    need("unit_ffn")

    def first(block, carry):
        rs = rows_at(block, half_rows)
        grad, unit_rows = grad_of(block), unit_of(block)
        factor = stats[rs, FACTOR_FFN : FACTOR_FFN + 1]
        sums["gain_ffn"][...] += column_sum(grad * unit_rows)
        sums["shift_ffn"][...] += column_sum(grad)
        grad_sum = norm_back(grad * vec["gain_ffn"][...], unit_rows, factor)
        gsum[rs, :] = grad_sum
        gouter[rs, :] = grad_sum.astype(bf16)
        sums["bias_back"][...] += column_sum(grad_sum)
        return carry

    lax.fori_loop(0, 2, first, 0)
    hook("first", 0)
    need("hidden")

    def hidden(j, carry):
        cs = rows_at(j, width)
        grad_inner = mm(gouter[...], w_back[cs, :], NT) * slope[:, cs].astype(f32)
        sums["bias_in"](j)[...] += column_sum(grad_inner)
        slope[:, cs] = grad_inner.astype(bf16)
        hook("hidden", j)
        return carry

    lax.fori_loop(0, w_in.shape[1] // width, hidden, 0)
    hook("hidden_end", 0)
    need("middle")

    def middle(block, carry):
        rs = rows_at(block, half_rows)
        grad = gsum[rs, :] + mm(slope[rs, :], w_in[...], NT)
        unit_rows = unit[rs, :]
        factor = stats[rs, FACTOR_ATTN : FACTOR_ATTN + 1]
        sums["gain_attn"][...] += column_sum(grad * unit_rows)
        sums["shift_attn"][...] += column_sum(grad)
        grad_sum = norm_back(grad * vec["gain_attn"][...], unit_rows, factor)
        gsum[rs, :] = grad_sum
        rounded = grad_sum.astype(bf16)
        gatt[rs, :] = rounded
        sums["bias_out"][...] += column_sum(grad_sum)
        gmix[rs, :] = mm(rounded, w_out[...], NT).astype(bf16)
        hook("middle", block)
        return carry

    lax.fori_loop(0, 2, middle, 0)
    hook("middle_end", 0)
    need("attention")
    attention_backward(
        qkv, gmix, mixed, stats, length, width, sums, lambda h: hook("attention", h)
    )
    hook("attention_end", 0)
    need("last")

    def last(block, carry):
        rs = rows_at(block, half_rows)
        give(block, gsum[rs, :] + mm(qkv[rs, :], w_qkv[...], NT))
        hook("last", block)
        return carry

    lax.fori_loop(0, 2, last, 0)


def layer_kernel(chips, *refs):
    (x_in, cotangent, w_qkv, w_out, w_in, w_back), refs = refs[:6], refs[6:]
    vec, refs = dict(zip(FORWARD_VECTORS, refs)), refs[len(FORWARD_VECTORS) :]
    lengths, refs = refs[0], refs[1:]
    acts_out, grad_out, blocks_out, sums_out, units_out, refs = *refs[:5], refs[5:]
    weights, refs = refs[:4], refs[4:]
    x_kept, qkv, mixed, stats, slope, active, normed, refs = *refs[:7], refs[7:]
    gouter, gatt, gmix, gsend, gsum, unit, totals, total_slots, refs = *refs[:8], refs[8:]
    acc_first, slots, refs = *refs[:2], refs[2:]
    weight_sem, x_sem, g_sem, unit_sem, acts_sem, forth_send, forth_recv, refs = *refs[:7], refs[7:]
    back_send, back_recv, grad_sem, sib_send, sib_recv, sib_free, refs = *refs[:6], refs[6:]
    ring_send, ring_recv, share_send, share_recv, sum_send, sum_recv, refs = *refs[:6], refs[6:]
    out_sem, sum_out_sem = refs
    rank = lax.axis_index("section")
    me = lax.axis_index("dp")
    peer = (1 - rank, me)
    rows, width = gsum.shape
    half_rows = rows // 2

    core = lax.rem(me, 2)
    chip = lax.div(me, 2)
    ring_half = chips // 2
    place = jnp.where(lax.rem(chip, 2) == 0, lax.div(chip, 2), chips - 1 - lax.div(chip, 2))
    rounds, _, subs = ring_recv.shape[:3]
    piece = -(-width // (16 * subs * chips)) * 16 * subs
    part = piece // subs
    steps = chips - 1
    bits = total_slots.shape[0]

    def device_at(position):
        position = lax.rem(position + chips, chips)
        spot = jnp.where(position < ring_half, 2 * position, 2 * (chips - 1 - position) + 1)
        return (rank, 2 * spot + core)

    sibling = (rank, me + 1 - 2 * core)
    ways = (device_at(place + 1), device_at(place - 1))

    def across(bit):
        size = 1 << bit
        return (rank, me + size - 2 * size * lax.rem(lax.div(me, size), 2))

    def half_at(i, block):
        return pl.ds(pl.multiple_of(i * rows + block * half_rows, half_rows), half_rows)

    query = pl.ds(0, width)
    key_value = pl.ds(width, 2 * width)
    loads = dict(
        query=(w_qkv.at[0, :, query], weights[0].at[:, query]),
        key=(w_qkv.at[0, :, key_value], weights[0].at[:, key_value]),
        out=(w_out.at[0], weights[1]),
        back=(w_back.at[0], weights[3]),
    )
    loads["in"] = (w_in.at[0], weights[2])
    order = ("query", "key", "out", "in", "back")
    loads = {
        name: pltpu.make_async_copy(*loads[name], weight_sem.at[k]) for k, name in enumerate(order)
    }

    def x_load(i):
        rs = rows_at(i, rows)
        return pltpu.make_async_copy(x_in.at[rs], x_kept.at[rs], x_sem.at[i])

    def g_load():
        return pltpu.make_async_copy(cotangent, gouter, g_sem)

    @pl.when(rank == 0)
    def _():
        x_load(0).start()

    loads["query"].start()
    loads["key"].start()
    barrier = pltpu.get_barrier_semaphore()
    partners = [peer, sibling, *ways] + [across(bit) for bit in range(1, bits)]
    for partner in partners:
        pl.semaphore_signal(barrier, inc=1, device_id=partner, device_id_type=MESH)
    totals[...] = jnp.zeros_like(totals)
    sums = {name: totals.at[pl.ds(k, 1)] for k, name in enumerate(SUM_ROWS)}
    sums["bias_in"] = lambda j: totals.at[pl.ds(len(SUM_ROWS) + j, 1)]
    pl.semaphore_wait(barrier, len(partners))

    def forth(i, block):
        rs = half_at(i, block)
        return pltpu.make_async_remote_copy(
            src_ref=gatt.at[rs],
            dst_ref=x_kept.at[rs],
            send_sem=forth_send.at[i, block],
            recv_sem=forth_recv.at[i, block],
            device_id=peer,
            device_id_type=MESH,
        )

    def acts_copy(i):
        rs = rows_at(i, rows)
        return pltpu.make_async_copy(gatt.at[rs], acts_out.at[rs], acts_sem.at[i])

    def spill(k):
        return pltpu.make_async_copy((unit, gsum)[k], units_out.at[k], unit_sem.at[k])

    def unspill(k):
        return pltpu.make_async_copy(units_out.at[k], unit, unit_sem.at[k])

    def forward_batch(i, carry):
        mine = rows_at(i, rows)

        @pl.when(rank == 0)
        def _():
            x_load(i).wait()

        @pl.when(rank == 1)
        def _():
            forth(i, 0).wait_recv()
            forth(i, 1).wait_recv()

        def need(what):
            @pl.when(i == 0)
            def _():
                loads[what].wait()
                if what == "key":
                    loads["out"].start()
                    loads["in"].start()
                if what == "out":
                    loads["back"].start()

                    @pl.when(rank == 0)
                    def _():
                        x_load(1).start()

                    @pl.when(rank == 1)
                    def _():
                        g_load().start()

            if what in ("out", "back"):

                @pl.when(i > 0)
                def _():
                    spill(0 if what == "out" else 1).wait()

        def done(what):
            @pl.when(i < MB - 1)
            def _():
                spill(0 if what == "attn" else 1).start()

            if what == "ffn":
                acts_copy(i).start()

        def send(block):
            @pl.when(rank == 0)
            def _():
                forth(i, block).start()

        forward_block(
            weights,
            vec,
            need,
            lengths[i],
            [ref.at[mine] for ref in (x_kept, qkv, mixed, stats, slope, active, normed)],
            unit,
            gsum,
            gatt.at[mine],
            send,
            done,
        )
        return carry

    lax.fori_loop(0, MB, forward_batch, 0)

    def acc(r, way, rs=None):
        rs = pl.ds(0, width) if rs is None else rs
        if r == 0:
            return acc_first.at[way, rs]
        return weights[3].at[pl.ds(pl.multiple_of((2 * r - 2 + way) * width + rs.start, 16), rs.size)]

    def term(r, owner, way):
        j = 2 * owner + way
        cs = rows_at(j, width)
        if r == 0:
            return mm(active[:, cs], gouter[...], TN)
        return mm(normed[...], slope[:, cs], TN)

    def sibling_term(r, way):
        if r == 0:
            return slots.at[1, way]
        return active.at[pl.ds(0, width), rows_at(way, width)]

    def to_sibling(r, way):
        return pltpu.make_async_remote_copy(
            src_ref=acc(r, way),
            dst_ref=sibling_term(r, way),
            send_sem=sib_send.at[way],
            recv_sem=sib_recv.at[way],
            device_id=sibling,
            device_id_type=MESH,
        )

    def compute_into(r, owner, way, put):
        if r < 2:
            put(term(r, owner, way))
            return
        j = 2 * owner + way

        @pl.when(j == 0)
        def _():
            put(mm(mixed[...], gatt[...], TN))

        @pl.when(j > 0)
        def _():
            put(mm(x_kept[...], qkv[:, rows_at(jnp.maximum(j - 1, 0), width)], TN))

    def compute(r, between=lambda: None):
        if r > 0:
            pl.semaphore_wait(sib_free, 1)

        def for_sibling(way, carry):
            def put(value):
                acc(r, way)[...] = value.astype(bf16)

            compute_into(r, 1 - core, way, put)
            to_sibling(r, way).start()
            return carry

        lax.fori_loop(0, 2, for_sibling, 0)
        between()

        def for_me(way, carry):
            def put(value):
                acc(r, way)[...] = value.astype(bf16)

            to_sibling(r, way).wait_send()
            compute_into(r, core, way, put)
            return carry

        lax.fori_loop(0, 2, for_me, 0)
        for way in (0, 1):
            to_sibling(r, way).wait_recv()
            acc(r, way)[...] = (acc(r, way)[...].astype(f32) + sibling_term(r, way)[...].astype(f32)).astype(bf16)
        if r < rounds - 1:
            pl.semaphore_signal(sib_free, inc=1, device_id=sibling, device_id_type=MESH)

    def rows_of(way, sub, t):
        sign = 1 - 2 * way
        index = lax.rem(place - sign * t + 2 * chips, chips)
        return pl.ds(pl.multiple_of(index * piece + sub * part, 16), part)

    def ring(r, way, sub, t, target):
        return pltpu.make_async_remote_copy(
            src_ref=acc(r, way, rows_of(way, sub, t)),
            dst_ref=target,
            send_sem=ring_send.at[r, way, sub, lax.rem(t, 2)],
            recv_sem=ring_recv.at[r, way, sub, t],
            device_id=ways[way],
            device_id_type=MESH,
        )

    def adding(r, way, sub, t):
        return ring(r, way, sub, t, slots.at[r, way, rows_of(way, sub, t)])

    def handing(r, way, sub, t):
        return ring(r, way, sub, t, acc(r, way, rows_of(way, sub, t)))

    def share(r, way, rs):
        return pltpu.make_async_remote_copy(
            src_ref=acc(r, way, rs),
            dst_ref=blocks_out.at[4 * r + 2 * core + way, rs],
            send_sem=share_send.at[r, way],
            recv_sem=share_recv.at[r, way],
            device_id=sibling,
            device_id_type=MESH,
        )

    def place_out(r, way, rs):
        block = blocks_out.at[4 * r + 2 * core + way, rs]
        return pltpu.make_async_copy(acc(r, way, rs), block, out_sem.at[r, way])

    def when(condition, way, t, body):
        if chips * piece > width:
            condition = condition & (rows_of(way, 0, t).start < width)
        if condition is True:
            body()
        elif condition is not False:
            pl.when(condition)(body)

    def chain(r, way, sub, t):
        def sent():
            adding(r, way, sub, t - 2).wait_send()

        def added():
            adding(r, way, sub, t - 1).wait_recv()
            rs = rows_of(way, sub, t)
            acc(r, way, rs)[...] = (
                acc(r, way, rs)[...].astype(f32) + slots[r, way, rs].astype(f32)
            ).astype(bf16)

        def kept():
            handing(r, way, sub, t - 1).wait_recv()

        def whole():
            share(r, way, rows_of(way, sub, t)).start()
            place_out(r, way, rows_of(way, sub, t)).start()

        when((t >= 2) & (t <= 2 * steps + 1), way, t - 2, sent)
        when((t >= 1) & (t <= steps), way, t, added)
        when((t >= 0) & (t < steps), way, t, lambda: adding(r, way, sub, t).start())
        when((t > steps) & (t <= 2 * steps), way, t, kept)
        when((t >= steps) & (t < 2 * steps), way, t, lambda: handing(r, way, sub, t).start())
        when((t >= steps) & (t <= 2 * steps), way, t, whole)

    def slot(tick, offsets):
        for r, offset in enumerate(offsets):
            for sub in range(subs):
                for way in (0, 1):
                    chain(r, way, sub, tick - offset)

    def back(i, block):
        return pltpu.make_async_remote_copy(
            src_ref=gsend.at[rows_at(block, half_rows)],
            dst_ref=gouter.at[half_at(i, block)],
            send_sem=back_send.at[block],
            recv_sem=back_recv.at[i, block],
            device_id=peer,
            device_id_type=MESH,
        )

    def grad_copy(i, block):
        source = gsum.at[rows_at(block, half_rows)]
        return pltpu.make_async_copy(source, grad_out.at[half_at(i, block)], grad_sem.at[block])

    early = (0, 3, 7)
    early_ticks = 8

    def backward_batch(turn, carry):
        i = MB - 1 - turn
        mine = rows_at(i, rows)

        def need(what):
            if what == "unit_ffn":

                @pl.when((turn == 0) & (rank == 1))
                def _():
                    g_load().wait()

                @pl.when(turn > 0)
                def _():
                    unspill(1).wait()
                    for block in (0, 1):
                        grad_copy(MB - 1, block).wait()

            if what == "hidden":

                @pl.when(turn > 0)
                def _():
                    unspill(0).start()

            if what == "middle":

                @pl.when(turn == 0)
                def _():
                    for k in range(MB):
                        acts_copy(k).wait()

                        @pl.when(rank == 0)
                        def _():
                            for block in (0, 1):
                                forth(k, block).wait_send()

                @pl.when(turn > 0)
                def _():
                    unspill(0).wait()

            if what == "attention":

                @pl.when(turn == 0)
                def _():
                    unspill(1).start()

        def hook(what, k):
            now = (turn == MB - 1) & (rank == 0)

            def at(condition, tick, rounds_now):
                @pl.when(now & condition)
                def _():
                    slot(tick, early[:rounds_now])

            if what == "first":

                @pl.when(now)
                def _():
                    compute(0)
                    slot(0, early[:1])

            if what == "hidden":
                at(k == 3, 1, 1)
            if what == "hidden_end":

                @pl.when(now)
                def _():
                    compute(1, lambda: slot(2, early[:1]))
                    slot(3, early[:2])

            if what == "middle":
                at(k == 1, 4, 2)
            if what == "attention" and k == 3:
                at(True, 5, 2)
            if what == "attention_end":

                @pl.when(now)
                def _():
                    compute(2, lambda: slot(6, early[:2]))
                    slot(7, early)

        def grad_of(block):
            @pl.when(rank == 0)
            def _():
                back(i, block).wait_recv()

            return gouter[half_at(i, block), :].astype(f32)

        def unit_of(block):
            rs = rows_at(block, half_rows)
            return jnp.where(turn == 0, gsum[rs, :], unit[rs, :])

        def give(block, value):
            @pl.when((turn > 0) & (rank == 1))
            def _():
                back(MB - 1, block).wait_send()

            rs = rows_at(block, half_rows)
            rounded = value.astype(bf16)
            gsend[rs, :] = rounded
            gsum[rs, :] = jnp.where(rank == 1, rounded.astype(f32), value)
            grad_copy(i, block).start()

            @pl.when(rank == 1)
            def _():
                back(i, block).start()

        backward_block(
            grad_of,
            unit_of,
            weights,
            vec,
            need,
            lengths[i],
            [ref.at[mine] for ref in (qkv, mixed, stats, slope)],
            (unit, gouter.at[mine], gatt.at[mine], gmix, gsum),
            sums,
            give,
            hook,
        )
        return carry

    lax.fori_loop(0, MB, backward_batch, 0)

    def sum_step(bit):
        return pltpu.make_async_remote_copy(
            src_ref=totals,
            dst_ref=total_slots.at[bit],
            send_sem=sum_send.at[bit],
            recv_sem=sum_recv.at[bit],
            device_id=across(bit),
            device_id_type=MESH,
        )

    @pl.when(rank == 1)
    def _():
        compute(0)

    start = jnp.where(rank == 0, early_ticks, 0)
    offsets = [jnp.where(rank == 0, early[r], r) for r in range(rounds)]

    def rest(tick, carry):
        slot(tick, offsets)
        for r in range(1, rounds):

            @pl.when((rank == 1) & (tick == r - 1))
            def _():
                compute(r)

        for bit in range(bits + 1):

            @pl.when(tick - start == 2 + bit)
            def _():
                if bit > 0:
                    sum_step(bit - 1).wait()
                    totals[...] += total_slots[bit - 1]
                if bit < bits:
                    sum_step(bit).start()

        return carry

    lax.fori_loop(start, offsets[-1] + 2 * steps + 2, rest, 0)
    sum_copy = pltpu.make_async_copy(totals, sums_out, sum_out_sem)
    sum_copy.start()
    for block in (0, 1):
        grad_copy(0, block).wait()

        @pl.when(rank == 1)
        def _():
            back(0, block).wait_send()

    everything = pl.ds(0, width)
    for r in range(rounds):
        for way in (0, 1):
            share(r, way, everything).wait_recv()
            share(r, way, everything).wait_send()
            place_out(r, way, everything).wait()
    sum_copy.wait()


def finish_kernel(acts, grads, blocks, sums, *refs):
    acts_out, grads_out, refs = refs[0], refs[1], refs[2:]
    outs, vectors, refs = refs[:4], refs[4 : 4 + len(SUM_ROWS) + 1], refs[5 + len(SUM_ROWS) :]
    taken, wide, acts_kept, grads_kept, in_sem, out_sem, copy_sem = refs
    depth, width = taken.shape[0], sums.shape[1]
    ways = ((acts, acts_kept, acts_out), (grads, grads_kept, grads_out))
    copies_in = [
        pltpu.make_async_copy(source, kept, copy_sem.at[k])
        for k, (source, kept, _) in enumerate(ways)
    ]
    copies_out = [
        pltpu.make_async_copy(kept, out.at[0], copy_sem.at[k])
        for k, (_, kept, out) in enumerate(ways)
    ]

    def target(k):
        if k < 4:
            return outs[0].at[0, pl.ds(k * width, width)]
        if k < 8:
            return outs[1].at[0, :, pl.ds((k - 4) * width, width)]
        if k < 9:
            return outs[2].at[0]
        return outs[3].at[0, :, pl.ds((k - 9) * width, width)]

    def load(k):
        return pltpu.make_async_copy(blocks.at[k], taken.at[k % depth], in_sem.at[k % depth])

    def store(k):
        return pltpu.make_async_copy(wide.at[k % depth], target(k), out_sem.at[k % depth])

    count = blocks.shape[0]
    for k in range(depth):
        load(k).start()
    for copy in copies_in:
        copy.start()
    for k, out in enumerate(vectors[:-1]):
        out[...] = sums[k : k + 1, :]
    for j in range(vectors[-1].shape[1] // width):
        row = len(SUM_ROWS) + j
        vectors[-1][:, j * width : (j + 1) * width] = sums[row : row + 1, :]
    for k in range(count):
        load(k).wait()
        if k >= depth:
            store(k - depth).wait()
        wide[k % depth] = taken[k % depth].astype(f32)
        store(k).start()
        if k + depth < count:
            load(k + depth).start()
        elif k + depth == count:
            for copy_in, copy_out in zip(copies_in, copies_out):
                copy_in.wait()
                copy_out.start()
    for k in range(count - depth, count):
        store(k).wait()
    for copy in copies_out:
        copy.wait()


def per_device(chips, *args):
    x_input = args[0]
    names = (
        "w_qkv", "bias_query", "bias_value", "w_out", "bias_out", "gain_attn", "shift_attn",
        "w_in", "bias_in", "w_back", "bias_back", "gain_ffn", "shift_ffn",
    )
    given = dict(zip(names, args[1:14]))
    lengths, cotangent = args[14:]
    row_count, width = x_input.shape
    rows = row_count // MB
    hidden = given["w_in"].shape[2]
    weights = [given[name] for name in ("w_qkv", "w_out", "w_in", "w_back")]
    anywhere = pl.BlockSpec(memory_space=pl.ANY)
    vmem = pl.BlockSpec(memory_space=pltpu.VMEM)
    smem = pl.BlockSpec(memory_space=pltpu.SMEM)
    dma = pltpu.SemaphoreType.DMA
    shape = jax.ShapeDtypeStruct
    weight_scratch = [pltpu.VMEM(w.shape[1:], bf16) for w in weights]
    kept = [
        (width, bf16),
        (3 * width, bf16),
        (width, bf16),
        (LANES, f32),
        (hidden, bf16),
        (hidden, bf16),
        (width, bf16),
    ]
    rounds = (3 * width + width + 2 * hidden) // (4 * width)
    subs = 2 if width % (32 * chips) == 0 else 1
    steps = chips - 1
    bits = (2 * chips).bit_length() - 1
    square = (width, width)

    def whole_rows(columns):
        return [pltpu.VMEM((row_count, n), kind) for n, kind in columns]

    acts, input_grads, blocks, totals, _ = pl.pallas_call(
        functools.partial(layer_kernel, chips),
        out_shape=[
            shape((row_count, width), bf16),
            shape((row_count, width), f32),
            shape((4 * rounds, *square), bf16),
            shape((SUM_COUNT, width), f32),
            shape((2, rows, width), f32),
        ],
        in_specs=[anywhere] * 6 + [vmem] * len(FORWARD_VECTORS) + [smem],
        out_specs=[anywhere] * 5,
        scratch_shapes=weight_scratch
        + whole_rows(kept)
        + whole_rows([(width, bf16)] * 2)
        + [
            pltpu.VMEM((rows, width), bf16),
            pltpu.VMEM((rows, width), bf16),
            pltpu.VMEM((rows, width), f32),
            pltpu.VMEM((rows, width), f32),
            pltpu.VMEM((SUM_COUNT, width), f32),
            pltpu.VMEM((bits, SUM_COUNT, width), f32),
            pltpu.VMEM((2, *square), bf16),
            pltpu.VMEM((rounds, 2, *square), bf16),
            dma((5,)),
            dma((MB,)),
            dma,
            dma((2,)),
            dma((MB,)),
            dma((MB, 2)),
            dma((MB, 2)),
            dma((2,)),
            dma((MB, 2)),
            dma((2,)),
            dma((2,)),
            dma((2,)),
            pltpu.SemaphoreType.REGULAR,
            dma((rounds, 2, subs, 2)),
            dma((rounds, 2, subs, 2 * steps)),
            dma((rounds, 2)),
            dma((rounds, 2)),
            dma((bits,)),
            dma((bits,)),
            dma((rounds, 2)),
            dma,
        ],
        compiler_params=pltpu.CompilerParams(
            collective_id=0, has_side_effects=True, vmem_limit_bytes=VMEM_LIMIT
        ),
        name="layer",
    )(x_input, cotangent, *weights, *[given[name] for name in FORWARD_VECTORS], lengths)
    vector_names = SUM_ROWS + ("bias_in",)
    depth = 4
    acts, input_grads, *whole = pl.pallas_call(
        finish_kernel,
        out_shape=[
            shape((1, row_count, width), bf16),
            shape((1, row_count, width), f32),
            shape((1, hidden, width), f32),
            shape((1, width, hidden), f32),
            shape((1, width, width), f32),
            shape((1, width, 3 * width), f32),
        ]
        + [shape(given[name].shape, f32) for name in vector_names],
        in_specs=[anywhere] * 3 + [vmem],
        out_specs=[anywhere] * 6 + [vmem] * len(vector_names),
        scratch_shapes=[
            pltpu.VMEM((depth, *square), bf16),
            pltpu.VMEM((depth, *square), f32),
            pltpu.VMEM((row_count, width), bf16),
            pltpu.VMEM((row_count, width), f32),
            dma((depth,)),
            dma((depth,)),
            dma((2,)),
        ],
        compiler_params=pltpu.CompilerParams(vmem_limit_bytes=VMEM_LIMIT),
        name="finish",
    )(acts, input_grads, blocks, totals)
    grads = dict(zip(("w_back", "w_in", "w_out", "w_qkv") + vector_names, whole))
    return (acts, input_grads, *[grads[name] for name in names])


def solution(mesh):
    return jax.shard_map(
        functools.partial(per_device, mesh.shape["dp"] // 2),
        mesh=mesh,
        in_specs=(
            P("dp", None),
            P("section", None, None),
            P("section", None),
            P("section", None),
            P("section", None, None),
            P("section", None),
            P("section", None),
            P("section", None),
            P("section", None, None),
            P("section", None),
            P("section", None, None),
            P("section", None),
            P("section", None),
            P("section", None),
            P("dp"),
            P("dp", None),
        ),
        out_specs=(
            P("section", "dp", None),
            P("section", "dp", None),
            P("section", None, None),
            P("section", None),
            P("section", None),
            P("section", None, None),
            P("section", None),
            P("section", None),
            P("section", None),
            P("section", None, None),
            P("section", None),
            P("section", None, None),
            P("section", None),
            P("section", None),
            P("section", None),
        ),
        check_vma=False,
    )
```

profile of v0, /device:TPU:0, one launch (start us, length us, event | category | flops | bytes accessed | tf_op | source)
XLA Modules:
  0.0 324.1 jit_solution(3033933255645545570)
XLA Ops:
  0.7 305.1 %layer.1 = (bf16[1024,768]{1,0:T(8,128)(2,1)}, f32[1024,768]{1,0:T(8,128)}, bf16[12,768,768]{2,1,0:T(8,128)(2,1)}, f32[16,768]{1,0:T(8,128)}, f32[2,512,768]{2,1,0:T(8,128)}) custom-call(bf16[1024,768]{1,0:T(8,128)(2,1)} %refs_0_.1, bf16[1024,768]{1,0:T(8,128)(2,1)} %refs_1_.1, bf16[1,768,2304]{2,1,0:T(8,128)(2,1)} %refs_2_.1, bf16[1,768,768]{2,1,0:T(8,128)(2,1)} %refs_3_.1, ...), custom_call_target="tpu_custom_call" | custom-call | tf_op jit(solution)/shard_map/layer/pallas_call | solution.py:900
  305.8 18.1 %finish.1 = (bf16[1,1024,768]{2,1,0:T(8,128)(2,1)}, f32[1,1024,768]{2,1,0:T(8,128)}, f32[1,3072,768]{2,1,0:T(8,128)}, f32[1,768,3072]{2,1,0:T(8,128)}, f32[1,768...) custom-call(bf16[1024,768]{1,0:T(8,128)(2,1)} %get-tuple-element.34., ...), custom_call_target="tpu_custom_call" | custom-call | tf_op jit(solution)/shard_map/finish/pallas_call | solution.py:952
where the time goes:
time: 331 us; the launch traced here: 324 us
  Pallas kernels  323 us (98%)
    pallas_call x1, Pallas kernels, per_device(): pl.pallas_call(functools.partial(layer_kernel, chips), out_shape=[shape((...  305 us
    pallas_call x1, Pallas kernels, per_device(): pl.pallas_call(finish_kernel, out_shape=[shape((1, row_count, width), bf1...  18.1 us

commit v1 on v0

--- a/solution.py
+++ b/solution.py
@@ -15,6 +15,8 @@
 FACTOR_ATTN = 12
 FACTOR_FFN = 13
 STAT_COLUMNS = 16
+TURN_PAIRS = 2
+FORWARD_PAIRS = 3
 VMEM_LIMIT = 62 << 20
 
 FORWARD_VECTORS = (
@@ -43,6 +45,12 @@
     return lax.dot_general(left, right, dims, preferred_element_type=f32)
 
 
+def only_if(condition):
+    if isinstance(condition, bool):
+        return (lambda body: body()) if condition else (lambda body: None)
+    return pl.when(condition)
+
+
 def rows_at(index, count):
     return pl.ds(pl.multiple_of(index * count, count), count)
 
@@ -78,45 +86,51 @@
     return jnp.where(key < length, 0.0, DEAD).astype(bf16)
 
 
-def attention_forward(qkv, mixed, stats, length, width):
+def attention_forward(qkv, mixed, stats, logs, length, width):
     rows = qkv.shape[0]
-    heads = width // HEAD
     lane = lax.broadcasted_iota(jnp.int32, (rows, LANES), 1)
     dead = key_bias(rows, length)
     zero = jnp.zeros((rows, LANES), bf16)
     one = jnp.ones((rows, LANES), bf16)
 
-    def marked(part, head, mark):
-        value = qkv[:, pl.ds(part * width + head // 2 * LANES, LANES)]
-        own = (lane < HEAD) if head % 2 == 0 else (lane >= HEAD)
-        return jnp.where(own, value, jnp.where(lane == HEAD - HEAD * (head % 2), mark, zero))
-
-    def scores_of(head):
-        return mm(marked(1, head, dead), marked(0, head, one), NT)
-
-    ahead = [scores_of(0), scores_of(1)]
-    outs, log_totals = [], []
-    for head in range(heads):
-        if head + 2 < heads:
-            ahead.append(scores_of(head + 2))
-        scores = ahead[head]
-        ahead[head] = None
-        highest = jnp.max(scores, axis=0, keepdims=True)
-        weights = jnp.exp(scores - highest).astype(bf16)
-        product = mm(marked(2, head, one).T, weights)
-        odd = head % 2
-        total = product[HEAD - HEAD * odd : HEAD - HEAD * odd + 1]
-        outs.append(product[HEAD * odd : HEAD * odd + HEAD] * (1.0 / total))
-        log_totals.append(highest + jnp.log(total))
-        if odd:
-            mixed[:, pl.ds(head // 2 * LANES, LANES)] = jnp.concatenate(outs, 0).T.astype(bf16)
-            outs = []
-    spare = STAT_COLUMNS - heads
-    log_totals = jnp.concatenate(log_totals + [jnp.zeros((spare, rows), f32)], 0)
-    stats[:, :STAT_COLUMNS] = log_totals.T
-
-
-def forward_block(weights, vec, need, length, saved, unit1, unit2, result, send, done):
+    def turn_of(turn, carry):
+        def columns(part, head):
+            at = part * width + (turn * FORWARD_PAIRS + head // 2) * LANES
+            return pl.ds(pl.multiple_of(at, LANES), LANES)
+
+        def marked(part, head, mark):
+            own = (lane < HEAD) if head % 2 == 0 else (lane >= HEAD)
+            mark = jnp.where(lane == HEAD - HEAD * (head % 2), mark, zero)
+            return jnp.where(own, qkv[:, columns(part, head)], mark)
+
+        def scores_of(head):
+            return mm(marked(1, head, dead), marked(0, head, one), NT)
+
+        heads = 2 * FORWARD_PAIRS
+        ahead = [scores_of(0), scores_of(1)]
+        outs = []
+        for head in range(heads):
+            if head + 2 < heads:
+                ahead.append(scores_of(head + 2))
+            scores = ahead[head]
+            ahead[head] = None
+            highest = jnp.max(scores, axis=0, keepdims=True)
+            weights = jnp.exp(scores - highest).astype(bf16)
+            product = mm(marked(2, head, one).T, weights)
+            odd = head % 2
+            total = product[HEAD - HEAD * odd : HEAD - HEAD * odd + 1]
+            outs.append(product[HEAD * odd : HEAD * odd + HEAD] * (1.0 / total))
+            logs[pl.ds(turn * heads + head, 1), :] = highest + jnp.log(total)
+            if odd:
+                mixed[:, columns(0, head)] = jnp.concatenate(outs, 0).T.astype(bf16)
+                outs = []
+        return carry
+
+    lax.fori_loop(0, width // (FORWARD_PAIRS * LANES), turn_of, 0)
+    stats[:, :STAT_COLUMNS] = logs[...].T
+
+
+def forward_block(weights, vec, need, length, saved, logs, unit1, unit2, result, send, done):
     w_qkv, w_out, w_in, w_back = weights
     x, qkv, mixed, stats, slope, active, normed = saved
     rows, width = x.shape
@@ -127,7 +141,7 @@
     need("key")
     qkv[:, width : 2 * width] = mm(x[...], w_qkv[:, width : 2 * width]).astype(bf16)
     qkv[:, 2 * width :] = (mm(x[...], w_qkv[:, 2 * width :]) + vec["bias_value"][...]).astype(bf16)
-    attention_forward(qkv, mixed, stats, length, width)
+    attention_forward(qkv, mixed, stats, logs, length, width)
     lane = lax.broadcasted_iota(jnp.int32, (half_rows, LANES), 1)
     need("out")
 
@@ -173,56 +187,64 @@
 
 def attention_backward(qkv, gmix, mixed, stats, length, width, sums, between):
     rows = qkv.shape[0]
-    heads = width // HEAD
     lane = lax.broadcasted_iota(jnp.int32, (rows, LANES), 1)
     dead = key_bias(rows, length)
     zero = jnp.zeros((rows, LANES), bf16)
     one = jnp.ones((rows, LANES), bf16)
 
-    def operands(head):
-        cols = [pl.ds(part * width + head // 2 * LANES, LANES) for part in range(3)]
-        q2, k2, v2 = [qkv[:, c] for c in cols]
-        g2 = gmix[:, cols[0]]
-        own = (lane < HEAD) if head % 2 == 0 else (lane >= HEAD)
-        at = HEAD - HEAD * (head % 2)
-        terms = jnp.where(own, g2.astype(f32) * mixed[:, cols[0]].astype(f32), 0.0)
-        d0, d1, d2 = split_three(-jnp.sum(terms, axis=-1, keepdims=True))
-        l0, l1, l2 = split_three(-stats[:, head : head + 1])
-        m0, m1, m2, m3 = [lane == at + t for t in range(4)]
-        m012 = m0 | m1 | m2
-        qa = jnp.where(
-            own,
-            q2,
-            jnp.where(m0, l0, jnp.where(m1, l1, jnp.where(m2, l2, jnp.where(m3, one, zero)))),
-        )
-        ga = jnp.where(own, g2, jnp.where(m0, d0, jnp.where(m1, d1, jnp.where(m2, d2, zero))))
-        ka = jnp.where(own, k2, jnp.where(m012, one, jnp.where(m3, dead, zero)))
-        va = jnp.where(own, v2, jnp.where(m012, one, zero))
-        first = HEAD * (head % 2)
-        return q2, g2, k2.T[first : first + HEAD], mm(ka, qa, NT), mm(va, ga, NT)
-
-    ahead = operands(0)
-    grads = []
-    for head in range(heads):
-        q2, g2, k2_t, scores, grad_probs = ahead
-        if head + 1 < heads:
-            ahead = operands(head + 1)
-        probs = jnp.exp(scores)
-        grad_scores = (probs * grad_probs).astype(bf16)
-        grads.append((mm(k2_t, grad_scores), mm(grad_scores, q2), mm(probs.astype(bf16), g2)))
-        if head % 2:
-            pair = head // 2
-            even, odd = grads
-            grads = []
-            grad_q = jnp.concatenate([even[0], odd[0]], 0).T * (HEAD ** -0.5)
-            grad_k = jnp.where(lane < HEAD, even[1], odd[1])
-            grad_v = jnp.where(lane < HEAD, even[2], odd[2])
-            for part, grad in enumerate((grad_q, grad_k, grad_v)):
-                qkv[:, pl.ds(part * width + pair * LANES, LANES)] = grad.astype(bf16)
-            cols = pl.ds(pair * LANES, LANES)
-            sums["bias_query"][:, cols] += column_sum(grad_q)
-            sums["bias_value"][:, cols] += column_sum(grad_v)
-            between(pair)
+    def turn_of(turn, carry):
+        heads = 2 * TURN_PAIRS
+
+        def columns(part, head):
+            at = part * width + (turn * TURN_PAIRS + head // 2) * LANES
+            return pl.ds(pl.multiple_of(at, LANES), LANES)
+
+        def operands(head):
+            q2, k2, v2 = [qkv[:, columns(part, head)] for part in range(3)]
+            g2, mixed2 = gmix[:, columns(0, head)], mixed[:, columns(0, head)]
+            own = (lane < HEAD) if head % 2 == 0 else (lane >= HEAD)
+            at = HEAD - HEAD * (head % 2)
+            terms = jnp.where(own, g2.astype(f32) * mixed2.astype(f32), 0.0)
+            logs = jnp.where(lane == turn * heads + head, stats[...], 0.0)
+            d0, d1, d2 = split_three(-jnp.sum(terms, axis=-1, keepdims=True))
+            l0, l1, l2 = split_three(-jnp.sum(logs, axis=-1, keepdims=True))
+            m0, m1, m2, m3 = [lane == at + t for t in range(4)]
+            m012 = m0 | m1 | m2
+            qa = jnp.where(
+                own,
+                q2,
+                jnp.where(m0, l0, jnp.where(m1, l1, jnp.where(m2, l2, jnp.where(m3, one, zero)))),
+            )
+            ga = jnp.where(own, g2, jnp.where(m0, d0, jnp.where(m1, d1, jnp.where(m2, d2, zero))))
+            ka = jnp.where(own, k2, jnp.where(m012, one, jnp.where(m3, dead, zero)))
+            va = jnp.where(own, v2, jnp.where(m012, one, zero))
+            first = HEAD * (head % 2)
+            return q2, g2, k2.T[first : first + HEAD], mm(ka, qa, NT), mm(va, ga, NT)
+
+        ahead = operands(0)
+        grads = []
+        for head in range(heads):
+            q2, g2, k2_t, scores, grad_probs = ahead
+            if head + 1 < heads:
+                ahead = operands(head + 1)
+            probs = jnp.exp(scores)
+            grad_scores = (probs * grad_probs).astype(bf16)
+            grads.append((mm(k2_t, grad_scores), mm(grad_scores, q2), mm(probs.astype(bf16), g2)))
+            if head % 2:
+                even, odd = grads
+                grads = []
+                grad_q = jnp.concatenate([even[0], odd[0]], 0).T * (HEAD ** -0.5)
+                grad_k = jnp.where(lane < HEAD, even[1], odd[1])
+                grad_v = jnp.where(lane < HEAD, even[2], odd[2])
+                for part, grad in enumerate((grad_q, grad_k, grad_v)):
+                    qkv[:, columns(part, head)] = grad.astype(bf16)
+                cols = columns(0, head)
+                sums["bias_query"][:, cols] += column_sum(grad_q)
+                sums["bias_value"][:, cols] += column_sum(grad_v)
+        between(turn)
+        return carry
+
+    lax.fori_loop(0, width // (TURN_PAIRS * LANES), turn_of, 0)
 
 
 def backward_block(grad_of, unit_of, weights, vec, need, length, saved, work, sums, give, hook):
@@ -301,9 +323,9 @@
     lengths, refs = refs[0], refs[1:]
     acts_out, grad_out, blocks_out, sums_out, units_out, refs = *refs[:5], refs[5:]
     weights, refs = refs[:4], refs[4:]
-    x_kept, qkv, mixed, stats, slope, active, normed, refs = *refs[:7], refs[7:]
-    gouter, gatt, gmix, gsend, gsum, unit, totals, total_slots, refs = *refs[:8], refs[8:]
-    acc_first, slots, refs = *refs[:2], refs[2:]
+    mixed_x, attended_qkv, stats, slope, active, normed, refs = *refs[:6], refs[6:]
+    gouter, gmix, gsend, gsum, unit, totals, total_slots, refs = *refs[:7], refs[7:]
+    logs, acc_first, slots, refs = *refs[:3], refs[3:]
     weight_sem, x_sem, g_sem, unit_sem, acts_sem, forth_send, forth_recv, refs = *refs[:7], refs[7:]
     back_send, back_recv, grad_sem, sib_send, sib_recv, sib_free, refs = *refs[:6], refs[6:]
     ring_send, ring_recv, share_send, share_recv, sum_send, sum_recv, refs = *refs[:6], refs[6:]
@@ -313,6 +335,9 @@
     peer = (1 - rank, me)
     rows, width = gsum.shape
     half_rows = rows // 2
+    mixed, x_kept = [mixed_x.at[:, pl.ds(k * width, width)] for k in range(2)]
+    gatt = attended_qkv.at[:, pl.ds(0, width)]
+    qkv = attended_qkv.at[:, pl.ds(width, 3 * width)]
 
     core = lax.rem(me, 2)
     chip = lax.div(me, 2)
@@ -451,6 +476,7 @@
             need,
             lengths[i],
             [ref.at[mine] for ref in (x_kept, qkv, mixed, stats, slope, active, normed)],
+            logs,
             unit,
             gsum,
             gatt.at[mine],
@@ -466,13 +492,6 @@
         if r == 0:
             return acc_first.at[way, rs]
         return weights[3].at[pl.ds(pl.multiple_of((2 * r - 2 + way) * width + rs.start, 16), rs.size)]
-
-    def term(r, owner, way):
-        j = 2 * owner + way
-        cs = rows_at(j, width)
-        if r == 0:
-            return mm(active[:, cs], gouter[...], TN)
-        return mm(normed[...], slope[:, cs], TN)
 
     def sibling_term(r, way):
         if r == 0:
@@ -489,47 +508,61 @@
             device_id_type=MESH,
         )
 
-    def compute_into(r, owner, way, put):
-        if r < 2:
-            put(term(r, owner, way))
-            return
+    def compute_into(r, owner, way, tile):
         j = 2 * owner + way
-
-        @pl.when(j == 0)
-        def _():
-            put(mm(mixed[...], gatt[...], TN))
-
-        @pl.when(j > 0)
-        def _():
-            put(mm(x_kept[...], qkv[:, rows_at(jnp.maximum(j - 1, 0), width)], TN))
+        here = pl.ds(pl.multiple_of(tile * tile_rows, tile_rows), tile_rows)
+        there = acc(r, way, here)
+
+        left, at, right = (
+            (active, j * width, gouter),
+            (normed, 0, slope.at[:, rows_at(j, width)]),
+            (mixed_x, jnp.minimum(j, 1) * width, attended_qkv.at[:, rows_at(j, width)]),
+        )[r]
+        cs = pl.ds(pl.multiple_of(at + tile * tile_rows, LANES), tile_rows)
+        there[...] = mm(left[:, cs], right[...], TN).astype(bf16)
+
+    tiles = 2
+    tile_rows = width // tiles
+    add_rows = 64
 
     def compute(r, between=lambda: None):
         if r > 0:
             pl.semaphore_wait(sib_free, 1)
 
-        def for_sibling(way, carry):
-            def put(value):
-                acc(r, way)[...] = value.astype(bf16)
-
-            compute_into(r, 1 - core, way, put)
-            to_sibling(r, way).start()
+        def for_sibling(step, carry):
+            way, tile = lax.div(step, tiles), lax.rem(step, tiles)
+            compute_into(r, 1 - core, way, tile)
+
+            @pl.when(tile == tiles - 1)
+            def _():
+                to_sibling(r, way).start()
+
             return carry
 
-        lax.fori_loop(0, 2, for_sibling, 0)
+        lax.fori_loop(0, 2 * tiles, for_sibling, 0)
         between()
 
-        def for_me(way, carry):
-            def put(value):
-                acc(r, way)[...] = value.astype(bf16)
-
-            to_sibling(r, way).wait_send()
-            compute_into(r, core, way, put)
+        def for_me(step, carry):
+            way, tile = lax.div(step, tiles), lax.rem(step, tiles)
+
+            @pl.when(tile == 0)
+            def _():
+                to_sibling(r, way).wait_send()
+
+            compute_into(r, core, way, tile)
             return carry
 
-        lax.fori_loop(0, 2, for_me, 0)
+        lax.fori_loop(0, 2 * tiles, for_me, 0)
         for way in (0, 1):
             to_sibling(r, way).wait_recv()
-            acc(r, way)[...] = (acc(r, way)[...].astype(f32) + sibling_term(r, way)[...].astype(f32)).astype(bf16)
+
+            def add(k, carry):
+                rs = rows_at(k, add_rows)
+                mine, other = acc(r, way, rs), sibling_term(r, way).at[rs]
+                mine[...] = (mine[...].astype(f32) + other[...].astype(f32)).astype(bf16)
+                return carry
+
+            lax.fori_loop(0, width // add_rows, add, 0)
         if r < rounds - 1:
             pl.semaphore_signal(sib_free, inc=1, device_id=sibling, device_id_type=MESH)
 
@@ -621,21 +654,21 @@
         source = gsum.at[rows_at(block, half_rows)]
         return pltpu.make_async_copy(source, grad_out.at[half_at(i, block)], grad_sem.at[block])
 
-    early = (0, 3, 7)
-    early_ticks = 8
-
-    def backward_batch(turn, carry):
+    early = (0, 3, 9)
+    early_ticks = 12
+
+    def backward_batch(turn, rank, hooked):
         i = MB - 1 - turn
         mine = rows_at(i, rows)
 
         def need(what):
             if what == "unit_ffn":
 
-                @pl.when((turn == 0) & (rank == 1))
+                @only_if((turn == 0) & (rank == 1))
                 def _():
                     g_load().wait()
 
-                @pl.when(turn > 0)
+                @only_if(turn > 0)
                 def _():
                     unspill(1).wait()
                     for block in (0, 1):
@@ -643,69 +676,65 @@
 
             if what == "hidden":
 
-                @pl.when(turn > 0)
+                @only_if(turn > 0)
                 def _():
                     unspill(0).start()
 
             if what == "middle":
 
-                @pl.when(turn == 0)
+                @only_if(turn == 0)
                 def _():
                     for k in range(MB):
                         acts_copy(k).wait()
 
-                        @pl.when(rank == 0)
+                        @only_if(rank == 0)
                         def _():
                             for block in (0, 1):
                                 forth(k, block).wait_send()
 
-                @pl.when(turn > 0)
+                @only_if(turn > 0)
                 def _():
                     unspill(0).wait()
 
             if what == "attention":
 
-                @pl.when(turn == 0)
+                @only_if(turn == 0)
                 def _():
                     unspill(1).start()
 
         def hook(what, k):
-            now = (turn == MB - 1) & (rank == 0)
+            if not hooked:
+                return
 
             def at(condition, tick, rounds_now):
-                @pl.when(now & condition)
+                @only_if(condition)
                 def _():
                     slot(tick, early[:rounds_now])
 
             if what == "first":
-
-                @pl.when(now)
-                def _():
-                    compute(0)
-                    slot(0, early[:1])
+                compute(0)
+                slot(0, early[:1])
 
             if what == "hidden":
                 at(k == 3, 1, 1)
             if what == "hidden_end":
-
-                @pl.when(now)
-                def _():
-                    compute(1, lambda: slot(2, early[:1]))
-                    slot(3, early[:2])
+                compute(1, lambda: slot(2, early[:1]))
+                slot(3, early[:2])
 
             if what == "middle":
                 at(k == 1, 4, 2)
-            if what == "attention" and k == 3:
-                at(True, 5, 2)
+            if what == "attention":
+                slot(5 + k, early[:2])
             if what == "attention_end":
-
-                @pl.when(now)
-                def _():
-                    compute(2, lambda: slot(6, early[:2]))
-                    slot(7, early)
+                compute(2, lambda: slot(8, early[:2]))
+                slot(9, early)
+
+            if what == "last":
+                at(k == 0, 10, 3)
+                at(k == 0, 11, 3)
 
         def grad_of(block):
-            @pl.when(rank == 0)
+            @only_if(rank == 0)
             def _():
                 back(i, block).wait_recv()
 
@@ -713,20 +742,25 @@
 
         def unit_of(block):
             rs = rows_at(block, half_rows)
+            if isinstance(turn, int):
+                return (gsum if turn == 0 else unit)[rs, :]
             return jnp.where(turn == 0, gsum[rs, :], unit[rs, :])
 
         def give(block, value):
-            @pl.when((turn > 0) & (rank == 1))
+            @only_if((turn > 0) & (rank == 1))
             def _():
                 back(MB - 1, block).wait_send()
 
             rs = rows_at(block, half_rows)
             rounded = value.astype(bf16)
             gsend[rs, :] = rounded
-            gsum[rs, :] = jnp.where(rank == 1, rounded.astype(f32), value)
+            if hooked:
+                gsum[rs, :] = value
+            else:
+                gsum[rs, :] = jnp.where(rank == 1, rounded.astype(f32), value)
             grad_copy(i, block).start()
 
-            @pl.when(rank == 1)
+            @only_if(rank == 1)
             def _():
                 back(i, block).start()
 
@@ -743,9 +777,17 @@
             give,
             hook,
         )
-        return carry
-
-    lax.fori_loop(0, MB, backward_batch, 0)
+
+    def plain(turn, carry):
+        backward_batch(turn, rank, False)
+        return carry
+
+    lax.fori_loop(0, jnp.where(rank == 0, MB - 1, MB), plain, 0)
+
+    @pl.when(rank == 0)
+    def _():
+        backward_batch(MB - 1, 0, True)
+
 
     def sum_step(bit):
         return pltpu.make_async_remote_copy(
@@ -757,21 +799,21 @@
             device_id_type=MESH,
         )
 
+    late = (0, 1, 2)
+
     @pl.when(rank == 1)
     def _():
         compute(0)
-
-    start = jnp.where(rank == 0, early_ticks, 0)
-    offsets = [jnp.where(rank == 0, early[r], r) for r in range(rounds)]
+        slot(0, late[:1])
+        compute(1)
+        slot(1, late[:2])
+        compute(2)
+
+    start = jnp.where(rank == 0, early_ticks, 2)
+    offsets = [jnp.where(rank == 0, early[r], late[r]) for r in range(rounds)]
 
     def rest(tick, carry):
         slot(tick, offsets)
-        for r in range(1, rounds):
-
-            @pl.when((rank == 1) & (tick == r - 1))
-            def _():
-                compute(r)
-
         for bit in range(bits + 1):
 
             @pl.when(tick - start == 2 + bit)
@@ -880,9 +922,8 @@
     shape = jax.ShapeDtypeStruct
     weight_scratch = [pltpu.VMEM(w.shape[1:], bf16) for w in weights]
     kept = [
-        (width, bf16),
-        (3 * width, bf16),
-        (width, bf16),
+        (2 * width, bf16),
+        (4 * width, bf16),
         (LANES, f32),
         (hidden, bf16),
         (hidden, bf16),
@@ -910,7 +951,7 @@
         out_specs=[anywhere] * 5,
         scratch_shapes=weight_scratch
         + whole_rows(kept)
-        + whole_rows([(width, bf16)] * 2)
+        + whole_rows([(width, bf16)])
         + [
             pltpu.VMEM((rows, width), bf16),
             pltpu.VMEM((rows, width), bf16),
@@ -918,6 +959,7 @@
             pltpu.VMEM((rows, width), f32),
             pltpu.VMEM((SUM_COUNT, width), f32),
             pltpu.VMEM((bits, SUM_COUNT, width), f32),
+            pltpu.VMEM((STAT_COLUMNS, rows), f32),
             pltpu.VMEM((2, *square), bf16),
             pltpu.VMEM((rounds, 2, *square), bf16),
             dma((5,)),

time: 331 us -> 312 us (0.943); the launches traced: 324 us -> 311 us
  Pallas kernels: 323 us -> 310 us
    pallas_call x1, Pallas kernels: 305 us -> 292 us  [per_device(): pl.pallas_call(functools.partial(layer_kernel, chips), out_shape=[shape((...]
where the time goes in v1:
time: 312 us; the launch traced here: 311 us
  Pallas kernels  310 us (99%)
    pallas_call x1, Pallas kernels, per_device(): pl.pallas_call(functools.partial(layer_kernel, chips), out_shape=[shape((...  292 us
    pallas_call x1, Pallas kernels, per_device(): pl.pallas_call(finish_kernel, out_shape=[shape((1, row_count, width), bf1...  18.1 us

profile of v1, /device:TPU:0, one launch (start us, length us, event | category | flops | bytes accessed | tf_op | source)
XLA Modules:
  0.0 311.3 jit_solution(83940736342487946)
XLA Ops:
  0.7 292.3 %layer.1 = (bf16[1024,768]{1,0:T(8,128)(2,1)}, f32[1024,768]{1,0:T(8,128)}, bf16[12,768,768]{2,1,0:T(8,128)(2,1)}, f32[16,768]{1,0:T(8,128)}, f32[2,512,768]{2,1,0:T(8,128)}) custom-call(bf16[1024,768]{1,0:T(8,128)(2,1)} %refs_0_.1, bf16[1024,768]{1,0:T(8,128)(2,1)} %refs_1_.1, bf16[1,768,2304]{2,1,0:T(8,128)(2,1)} %refs_2_.1, bf16[1,768,768]{2,1,0:T(8,128)(2,1)} %refs_3_.1, ...), custom_call_target="tpu_custom_call" | custom-call | tf_op jit(solution)/shard_map/layer/pallas_call | solution.py:941
  293.0 18.1 %finish.1 = (bf16[1,1024,768]{2,1,0:T(8,128)(2,1)}, f32[1,1024,768]{2,1,0:T(8,128)}, f32[1,3072,768]{2,1,0:T(8,128)}, f32[1,768,3072]{2,1,0:T(8,128)}, f32[1,768...) custom-call(bf16[1024,768]{1,0:T(8,128)(2,1)} %get-tuple-element.34., ...), custom_call_target="tpu_custom_call" | custom-call | tf_op jit(solution)/shard_map/finish/pallas_call | solution.py:994

commit v2 on v1

--- a/solution.py
+++ b/solution.py
@@ -15,8 +15,8 @@
 FACTOR_ATTN = 12
 FACTOR_FFN = 13
 STAT_COLUMNS = 16
-TURN_PAIRS = 2
-FORWARD_PAIRS = 3
+TURN_PAIRS = 6
+FORWARD_PAIRS = 6
 VMEM_LIMIT = 62 << 20
 
 FORWARD_VECTORS = (
@@ -126,7 +126,11 @@
                 outs = []
         return carry
 
-    lax.fori_loop(0, width // (FORWARD_PAIRS * LANES), turn_of, 0)
+    turns = width // (FORWARD_PAIRS * LANES)
+    if turns == 1:
+        turn_of(0, 0)
+    else:
+        lax.fori_loop(0, turns, turn_of, 0)
     stats[:, :STAT_COLUMNS] = logs[...].T
 
 
@@ -157,22 +161,22 @@
     lax.fori_loop(0, 2, after_attention, 0)
     done("attn")
     need("in")
-
-    def hidden(j, carry):
-        cs = rows_at(j, width)
-        inner = mm(normed[...], w_in[:, cs]) + vec["bias_in"][:, cs]
-        share = 0.5 * (1.0 + lax.erf(inner * 0.7071067811865476))
-        active[:, cs] = (inner * share).astype(bf16)
-        slope[:, cs] = (
-            share + inner * jnp.exp(-0.5 * inner * inner) * 0.3989422804014327
-        ).astype(bf16)
-        return carry
-
-    lax.fori_loop(0, w_in.shape[1] // width, hidden, 0)
     need("back")
 
-    def after_ffn(block, carry):
+    def ffn(block, carry):
         rs = rows_at(block, half_rows)
+
+        def hidden(j, carry):
+            cs = rows_at(j, width)
+            inner = mm(normed[rs, :], w_in[:, cs]) + vec["bias_in"][:, cs]
+            share = 0.5 * (1.0 + lax.erf(inner * 0.7071067811865476))
+            active[rs, cs] = (inner * share).astype(bf16)
+            slope[rs, cs] = (
+                share + inner * jnp.exp(-0.5 * inner * inner) * 0.3989422804014327
+            ).astype(bf16)
+            return carry
+
+        lax.fori_loop(0, w_in.shape[1] // width, hidden, 0)
         summed = normed[rs, :].astype(f32) + mm(active[rs, :], w_back[...]) + vec["bias_back"][...]
         unit, factor = norm_rows(summed)
         unit2[rs, :] = unit
@@ -181,7 +185,7 @@
         send(block)
         return carry
 
-    lax.fori_loop(0, 2, after_ffn, 0)
+    lax.fori_loop(0, 2, ffn, 0)
     done("ffn")
 
 
@@ -199,15 +203,20 @@
             at = part * width + (turn * TURN_PAIRS + head // 2) * LANES
             return pl.ds(pl.multiple_of(at, LANES), LANES)
 
+        def log_total(head):
+            if isinstance(turn, int):
+                return stats[:, turn * heads + head : turn * heads + head + 1]
+            logs = jnp.where(lane == turn * heads + head, stats[...], 0.0)
+            return jnp.sum(logs, axis=-1, keepdims=True)
+
         def operands(head):
             q2, k2, v2 = [qkv[:, columns(part, head)] for part in range(3)]
             g2, mixed2 = gmix[:, columns(0, head)], mixed[:, columns(0, head)]
             own = (lane < HEAD) if head % 2 == 0 else (lane >= HEAD)
             at = HEAD - HEAD * (head % 2)
             terms = jnp.where(own, g2.astype(f32) * mixed2.astype(f32), 0.0)
-            logs = jnp.where(lane == turn * heads + head, stats[...], 0.0)
             d0, d1, d2 = split_three(-jnp.sum(terms, axis=-1, keepdims=True))
-            l0, l1, l2 = split_three(-jnp.sum(logs, axis=-1, keepdims=True))
+            l0, l1, l2 = split_three(-log_total(head))
             m0, m1, m2, m3 = [lane == at + t for t in range(4)]
             m012 = m0 | m1 | m2
             qa = jnp.where(
@@ -241,10 +250,14 @@
                 cols = columns(0, head)
                 sums["bias_query"][:, cols] += column_sum(grad_q)
                 sums["bias_value"][:, cols] += column_sum(grad_v)
-        between(turn)
+                between(turn * TURN_PAIRS + head // 2)
         return carry
 
-    lax.fori_loop(0, width // (TURN_PAIRS * LANES), turn_of, 0)
+    turns = width // (TURN_PAIRS * LANES)
+    if turns == 1:
+        turn_of(0, 0)
+    else:
+        lax.fori_loop(0, turns, turn_of, 0)
 
 
 def backward_block(grad_of, unit_of, weights, vec, need, length, saved, work, sums, give, hook):
@@ -355,7 +368,8 @@
         return (rank, 2 * spot + core)
 
     sibling = (rank, me + 1 - 2 * core)
-    ways = (device_at(place + 1), device_at(place - 1))
+    def way_to(way):
+        return device_at(place + 1 - 2 * way)
 
     def across(bit):
         size = 1 << bit
@@ -392,7 +406,7 @@
     loads["query"].start()
     loads["key"].start()
     barrier = pltpu.get_barrier_semaphore()
-    partners = [peer, sibling, *ways] + [across(bit) for bit in range(1, bits)]
+    partners = [peer, sibling, way_to(0), way_to(1)] + [across(bit) for bit in range(1, bits)]
     for partner in partners:
         pl.semaphore_signal(barrier, inc=1, device_id=partner, device_id_type=MESH)
     totals[...] = jnp.zeros_like(totals)
@@ -440,8 +454,8 @@
                 if what == "key":
                     loads["out"].start()
                     loads["in"].start()
+                    loads["back"].start()
                 if what == "out":
-                    loads["back"].start()
 
                     @pl.when(rank == 0)
                     def _():
@@ -498,71 +512,61 @@
             return slots.at[1, way]
         return active.at[pl.ds(0, width), rows_at(way, width)]
 
-    def to_sibling(r, way):
+    tiles = 2
+    tile_rows = width // tiles
+    first_tile = jnp.minimum(lax.div(place * piece, tile_rows), tiles - 1)
+
+    def to_sibling(r, way, tile):
+        here = rows_at(tile, tile_rows)
         return pltpu.make_async_remote_copy(
-            src_ref=acc(r, way),
-            dst_ref=sibling_term(r, way),
-            send_sem=sib_send.at[way],
-            recv_sem=sib_recv.at[way],
+            src_ref=acc(r, way, here),
+            dst_ref=sibling_term(r, way).at[here],
+            send_sem=sib_send.at[way, tile],
+            recv_sem=sib_recv.at[way, tile],
             device_id=sibling,
             device_id_type=MESH,
         )
 
-    def compute_into(r, owner, way, tile):
+    def term(r, owner, way, tile):
         j = 2 * owner + way
-        here = pl.ds(pl.multiple_of(tile * tile_rows, tile_rows), tile_rows)
-        there = acc(r, way, here)
-
         left, at, right = (
             (active, j * width, gouter),
             (normed, 0, slope.at[:, rows_at(j, width)]),
             (mixed_x, jnp.minimum(j, 1) * width, attended_qkv.at[:, rows_at(j, width)]),
         )[r]
         cs = pl.ds(pl.multiple_of(at + tile * tile_rows, LANES), tile_rows)
-        there[...] = mm(left[:, cs], right[...], TN).astype(bf16)
-
-    tiles = 2
-    tile_rows = width // tiles
-    add_rows = 64
-
-    def compute(r, between=lambda: None):
+        return mm(left[:, cs], right[...], TN)
+
+    def compute(r, between):
         if r > 0:
             pl.semaphore_wait(sib_free, 1)
 
-        def for_sibling(step, carry):
-            way, tile = lax.div(step, tiles), lax.rem(step, tiles)
-            compute_into(r, 1 - core, way, tile)
-
-            @pl.when(tile == tiles - 1)
+        def one_tile(step, carry):
+            tile = lax.rem(first_tile + step, tiles)
+            here = rows_at(tile, tile_rows)
+
+            def for_sibling(way, carry):
+                acc(r, way, here)[...] = term(r, 1 - core, way, tile).astype(bf16)
+                to_sibling(r, way, tile).start()
+                return carry
+
+            def for_me(way, carry):
+                value = term(r, core, way, tile)
+                to_sibling(r, way, tile).wait()
+                other = sibling_term(r, way).at[here]
+                acc(r, way, here)[...] = (value + other[...].astype(f32)).astype(bf16)
+                return carry
+
+            lax.fori_loop(0, 2, for_sibling, 0)
+            lax.fori_loop(0, 2, for_me, 0)
+
+            @pl.when(step == 0)
             def _():
-                to_sibling(r, way).start()
+                between()
 
             return carry
 
-        lax.fori_loop(0, 2 * tiles, for_sibling, 0)
-        between()
-
-        def for_me(step, carry):
-            way, tile = lax.div(step, tiles), lax.rem(step, tiles)
-
-            @pl.when(tile == 0)
-            def _():
-                to_sibling(r, way).wait_send()
-
-            compute_into(r, core, way, tile)
-            return carry
-
-        lax.fori_loop(0, 2 * tiles, for_me, 0)
-        for way in (0, 1):
-            to_sibling(r, way).wait_recv()
-
-            def add(k, carry):
-                rs = rows_at(k, add_rows)
-                mine, other = acc(r, way, rs), sibling_term(r, way).at[rs]
-                mine[...] = (mine[...].astype(f32) + other[...].astype(f32)).astype(bf16)
-                return carry
-
-            lax.fori_loop(0, width // add_rows, add, 0)
+        lax.fori_loop(0, tiles, one_tile, 0)
         if r < rounds - 1:
             pl.semaphore_signal(sib_free, inc=1, device_id=sibling, device_id_type=MESH)
 
@@ -577,7 +581,7 @@
             dst_ref=target,
             send_sem=ring_send.at[r, way, sub, lax.rem(t, 2)],
             recv_sem=ring_recv.at[r, way, sub, t],
-            device_id=ways[way],
+            device_id=way_to(way),
             device_id_type=MESH,
         )
 
@@ -636,9 +640,12 @@
 
     def slot(tick, offsets):
         for r, offset in enumerate(offsets):
-            for sub in range(subs):
-                for way in (0, 1):
-                    chain(r, way, sub, tick - offset)
+
+            def one_chain(k, carry):
+                chain(r, lax.rem(k, 2), lax.div(k, 2), tick - offset)
+                return carry
+
+            lax.fori_loop(0, 2 * subs, one_chain, 0)
 
     def back(i, block):
         return pltpu.make_async_remote_copy(
@@ -654,8 +661,8 @@
         source = gsum.at[rows_at(block, half_rows)]
         return pltpu.make_async_copy(source, grad_out.at[half_at(i, block)], grad_sem.at[block])
 
-    early = (0, 3, 9)
-    early_ticks = 12
+    early = (0, 4, 11)
+    early_ticks = 15
 
     def backward_batch(turn, rank, hooked):
         i = MB - 1 - turn
@@ -703,8 +710,14 @@
                     unspill(1).start()
 
         def hook(what, k):
-            if not hooked:
+            if what == "attention" and k % 2 == 0:
                 return
+
+            @only_if((turn == MB - 1) & (rank == 0))
+            def _():
+                ring_part(what, k)
+
+        def ring_part(what, k):
 
             def at(condition, tick, rounds_now):
                 @only_if(condition)
@@ -712,26 +725,23 @@
                     slot(tick, early[:rounds_now])
 
             if what == "first":
-                compute(0)
-                slot(0, early[:1])
-
+                compute(0, lambda: slot(0, early[:1]))
+                slot(1, early[:1])
             if what == "hidden":
-                at(k == 3, 1, 1)
+                at(lax.rem(k, 2) == 1, 2 + lax.div(k, 2), 1)
             if what == "hidden_end":
-                compute(1, lambda: slot(2, early[:1]))
-                slot(3, early[:2])
-
+                compute(1, lambda: slot(4, early[:2]))
+                slot(5, early[:2])
             if what == "middle":
-                at(k == 1, 4, 2)
-            if what == "attention":
-                slot(5 + k, early[:2])
+                slot(6 + k, early[:2])
+            if what == "attention" and k % 2 == 1:
+                slot(8 + k // 2, early[:2])
             if what == "attention_end":
-                compute(2, lambda: slot(8, early[:2]))
-                slot(9, early)
-
+                compute(2, lambda: slot(11, early))
+                slot(12, early)
+                slot(13, early)
             if what == "last":
-                at(k == 0, 10, 3)
-                at(k == 0, 11, 3)
+                at(k == 1, 14, 3)
 
         def grad_of(block):
             @only_if(rank == 0)
@@ -782,11 +792,7 @@
         backward_batch(turn, rank, False)
         return carry
 
-    lax.fori_loop(0, jnp.where(rank == 0, MB - 1, MB), plain, 0)
-
-    @pl.when(rank == 0)
-    def _():
-        backward_batch(MB - 1, 0, True)
+    lax.fori_loop(0, MB, plain, 0)
 
 
     def sum_step(bit):
@@ -799,17 +805,16 @@
             device_id_type=MESH,
         )
 
-    late = (0, 1, 2)
+    late = (0, 2, 4)
+    late_ticks = 6
 
     @pl.when(rank == 1)
     def _():
-        compute(0)
-        slot(0, late[:1])
-        compute(1)
-        slot(1, late[:2])
-        compute(2)
-
-    start = jnp.where(rank == 0, early_ticks, 2)
+        for r in range(rounds):
+            compute(r, lambda: slot(2 * r, late[: r + 1]))
+            slot(2 * r + 1, late[: r + 1])
+
+    start = jnp.where(rank == 0, early_ticks, late_ticks)
     offsets = [jnp.where(rank == 0, early[r], late[r]) for r in range(rounds)]
 
     def rest(tick, carry):
@@ -972,8 +977,8 @@
             dma((2,)),
             dma((MB, 2)),
             dma((2,)),
-            dma((2,)),
-            dma((2,)),
+            dma((2, 2)),
+            dma((2, 2)),
             pltpu.SemaphoreType.REGULAR,
             dma((rounds, 2, subs, 2)),
             dma((rounds, 2, subs, 2 * steps)),

time: 312 us -> 307 us (0.984)
  Pallas kernels: 310 us -> 306 us
    pallas_call x1, Pallas kernels: 292 us -> 288 us  [per_device(): pl.pallas_call(functools.partial(layer_kernel, chips), out_shape=[shape((...]
where the time goes in v2:
time: 307 us; the launch traced here: 306 us
  Pallas kernels  306 us (100%)
    pallas_call x1, Pallas kernels, per_device(): pl.pallas_call(functools.partial(layer_kernel, chips), out_shape=[shape((...  288 us
    pallas_call x1, Pallas kernels, per_device(): pl.pallas_call(finish_kernel, out_shape=[shape((1, row_count, width), bf1...  18.1 us

profile of v2, /device:TPU:0, one launch (start us, length us, event | category | flops | bytes accessed | tf_op | source)
XLA Modules:
  0.0 306.5 jit_solution(2705645470766946236)
XLA Ops:
  0.7 287.5 %layer.1 = (bf16[1024,768]{1,0:T(8,128)(2,1)}, f32[1024,768]{1,0:T(8,128)}, bf16[12,768,768]{2,1,0:T(8,128)(2,1)}, f32[16,768]{1,0:T(8,128)}, f32[2,512,768]{2,1,0:T(8,128)}) custom-call(bf16[1024,768]{1,0:T(8,128)(2,1)} %refs_0_.1, bf16[1024,768]{1,0:T(8,128)(2,1)} %refs_1_.1, bf16[1,768,2304]{2,1,0:T(8,128)(2,1)} %refs_2_.1, bf16[1,768,768]{2,1,0:T(8,128)(2,1)} %refs_3_.1, ...), custom_call_target="tpu_custom_call" | custom-call | tf_op jit(solution)/shard_map/layer/pallas_call | solution.py:946
  288.2 18.1 %finish.1 = (bf16[1,1024,768]{2,1,0:T(8,128)(2,1)}, f32[1,1024,768]{2,1,0:T(8,128)}, f32[1,3072,768]{2,1,0:T(8,128)}, f32[1,768,3072]{2,1,0:T(8,128)}, f32[1,768...) custom-call(bf16[1024,768]{1,0:T(8,128)(2,1)} %get-tuple-element.34., ...), custom_call_target="tpu_custom_call" | custom-call | tf_op jit(solution)/shard_map/finish/pallas_call | solution.py:999

commit v3 on v2

--- a/solution.py
+++ b/solution.py
@@ -935,7 +935,7 @@
         (width, bf16),
     ]
     rounds = (3 * width + width + 2 * hidden) // (4 * width)
-    subs = 2 if width % (32 * chips) == 0 else 1
+    subs = 3 if width % (48 * chips) == 0 else 1
     steps = chips - 1
     bits = (2 * chips).bit_length() - 1
     square = (width, width)

time: 307 us -> 305 us (level)
  no operation moved by 1% of the time
where the time goes in v3:
time: 305 us
  Pallas kernels  304 us (100%)
    pallas_call x1, Pallas kernels, per_device(): pl.pallas_call(functools.partial(layer_kernel, chips), out_shape=[shape((...  286 us
    pallas_call x1, Pallas kernels, per_device(): pl.pallas_call(finish_kernel, out_shape=[shape((1, row_count, width), bf1...  18.1 us

profile of v3, /device:TPU:0, one launch (start us, length us, event | category | flops | bytes accessed | tf_op | source)
XLA Modules:
  0.0 304.8 jit_solution(8976280393641099535)
XLA Ops:
  0.7 285.8 %layer.1 = (bf16[1024,768]{1,0:T(8,128)(2,1)}, f32[1024,768]{1,0:T(8,128)}, bf16[12,768,768]{2,1,0:T(8,128)(2,1)}, f32[16,768]{1,0:T(8,128)}, f32[2,512,768]{2,1,0:T(8,128)}) custom-call(bf16[1024,768]{1,0:T(8,128)(2,1)} %refs_0_.1, bf16[1024,768]{1,0:T(8,128)(2,1)} %refs_1_.1, bf16[1,768,2304]{2,1,0:T(8,128)(2,1)} %refs_2_.1, bf16[1,768,768]{2,1,0:T(8,128)(2,1)} %refs_3_.1, ...), custom_call_target="tpu_custom_call" | custom-call | tf_op jit(solution)/shard_map/layer/pallas_call | solution.py:946
  286.5 18.1 %finish.1 = (bf16[1,1024,768]{2,1,0:T(8,128)(2,1)}, f32[1,1024,768]{2,1,0:T(8,128)}, f32[1,3072,768]{2,1,0:T(8,128)}, f32[1,768,3072]{2,1,0:T(8,128)}, f32[1,768...) custom-call(bf16[1024,768]{1,0:T(8,128)(2,1)} %get-tuple-element.34., ...), custom_call_target="tpu_custom_call" | custom-call | tf_op jit(solution)/shard_map/finish/pallas_call | solution.py:999
